TPU v7x, 32 devices: a whole 2x2x4 slice. The times are simulated.
32 devices in a mesh: parts: 2 (over x), seq: 8 (over z, y), tp: 2 (over core).
Axes of the slice: x: 2, y: 2, z: 4, core: 2. Of those that a mesh axis runs over, the one named last changes fastest.
Arguments:
- video_q: bfloat16 [4096, 1024], P(('parts', 'seq', 'tp')), parts along dimension 0, may hold values from -6 to 6
- video_k: bfloat16 [4096, 1024], P(('parts', 'seq', 'tp')), parts along dimension 0, may hold values from -6 to 6
- video_v: bfloat16 [4096, 1024], P(('parts', 'seq', 'tp')), parts along dimension 0, may hold values from -6 to 6
- cross_q: bfloat16 [4096, 1024], P(('parts', 'seq', 'tp')), parts along dimension 0, may hold values from -6 to 6
- qk_gains: float32 [4, 1024], replicated, may hold values from 1 to 2
- captions: bfloat16 [4096, 4096], P(('parts', 'seq'), 'tp'), parts along dimension 0, may hold values from -16 to 16
- text_gain: float32 [4096], P('tp'), may hold values from 0.25 to 1.75
- cross_kv_weight: bfloat16 [4096, 2, 1024], P('tp', None, 'seq'), may hold values from -0.09375 to 0.09375
- lengths: int32 [8], P('parts'), parts along dimension 0, may hold values from 1 to 512, 1024 in all
- video_prompt: int32 [8], P('parts'), parts along dimension 0, may hold values from 0 to 3, each once
Outputs:
- self_out: bfloat16 [4096, 1024], P(('parts', 'seq', 'tp')), parts along dimension 0
- cross_out: bfloat16 [4096, 1024], P(('parts', 'seq', 'tp')), parts along dimension 0
There are 2 independent parts, one for each index of `parts`. A program takes and returns all parts, laid end to end along the dimension named above; an argument that names none is the same for every part. Nothing has to cross between parts.
Inputs may be any that keep to these rules, and one draw needn't show every extreme that they name: The lengths of a group's captions add up to 1024, and one caption has exactly 512. `video_prompt`: every caption belongs to exactly one video.
All inputs are finite; a program needn't handle non-finite values.
Results may differ from a plain program's by a relative error of at most 0.011.
Values may be sent and summed in bfloat16 or wider, within the bound.
A program may use at most 128 MiB of HBM per device.

v0:
```python
import math

import jax
import jax.numpy as jnp
from jax import lax
from jax.sharding import PartitionSpec as P

VIDEOS = 4
CAP = 512


EPS = 1e-06


def head_norm(rows, gain):
    values = rows.astype(jnp.float32)
    inverse = lax.rsqrt(jnp.mean(values * values, axis=-1, keepdims=True) + EPS)
    return (values * inverse * gain).astype(jnp.bfloat16)


def lookup(table, wanted):
    matches = wanted[..., None] == jnp.arange(table.shape[0], dtype=jnp.int32)
    return jnp.sum(jnp.where(matches, table, 0), axis=-1)


def per_device(
    video_q,
    video_k,
    video_v,
    cross_q,
    qk_gains,
    captions,
    text_gain,
    cross_kv_weight,
    lengths,
    video_prompt,
):
    tp_count = lax.axis_size("tp")
    seq_index = lax.axis_index("seq")
    head_dim = cross_kv_weight.shape[2]
    score_scale = 1.0 / math.sqrt(head_dim)
    head_gains = lax.dynamic_slice_in_dim(qk_gains, seq_index * head_dim, head_dim, 1)
    head_queries, head_keys, head_values, head_cross = (
        lax.all_to_all(video_q, "seq", split_axis=1, concat_axis=0, tiled=True),
        lax.all_to_all(video_k, "seq", split_axis=1, concat_axis=0, tiled=True),
        lax.all_to_all(video_v, "seq", split_axis=1, concat_axis=0, tiled=True),
        lax.all_to_all(cross_q, "seq", split_axis=1, concat_axis=0, tiled=True),
    )
    self_queries = head_norm(head_queries, head_gains[0])
    self_keys = head_norm(head_keys, head_gains[1])
    cross_queries = head_norm(head_cross, head_gains[2])
    all_keys, all_values = (
        lax.all_gather(self_keys, "tp", axis=0, tiled=True),
        lax.all_gather(head_values, "tp", axis=0, tiled=True),
    )
    caption_values = captions.astype(jnp.float32)
    square_sums = lax.psum(jnp.sum(caption_values * caption_values, axis=1), "tp")
    feature_total = captions.shape[1] * tp_count
    inverse = lax.rsqrt(square_sums / feature_total + EPS)
    text_normed = (caption_values * inverse[:, None] * text_gain[None, :]).astype(jnp.bfloat16)
    weight = cross_kv_weight.reshape(cross_kv_weight.shape[0], 2 * head_dim)
    gathered = jnp.dot(
        lax.all_gather(text_normed, "seq", axis=0, tiled=True),
        weight,
        preferred_element_type=jnp.float32,
    )
    key_value = lax.psum(gathered, "tp")
    first_rows = video_prompt * CAP
    cross_keys = head_norm(key_value[:, :head_dim], head_gains[3])
    cross_values = key_value[:, head_dim:].astype(jnp.bfloat16)
    video_lengths = lookup(lengths, video_prompt)
    row_count = self_queries.shape[0]
    half_len = row_count // VIDEOS
    query_blocks = self_queries.reshape(VIDEOS, half_len, head_dim)
    cross_blocks = cross_queries.reshape(VIDEOS, half_len, head_dim)
    key_blocks = jnp.swapaxes(all_keys.reshape(tp_count, VIDEOS, half_len, head_dim), 0, 1)
    value_blocks = jnp.swapaxes(all_values.reshape(tp_count, VIDEOS, half_len, head_dim), 0, 1)
    cap_index = jnp.arange(CAP, dtype=jnp.int32)

    def attend(operands):
        queries_v, keys_v, values_v, cross_v, first_row_v, length_v = operands
        keys_flat = keys_v.reshape(-1, head_dim)
        values_flat = values_v.reshape(-1, head_dim)
        scores = (
            jnp.einsum("qd,kd->qk", queries_v, keys_flat, preferred_element_type=jnp.float32)
            * score_scale
        )
        exp_scores = jnp.exp(scores)
        weights = (exp_scores / jnp.sum(exp_scores, axis=1, keepdims=True)).astype(jnp.bfloat16)
        self_part = jnp.dot(weights, values_flat, preferred_element_type=jnp.float32).astype(
            jnp.bfloat16
        )
        cap_keys = lax.dynamic_slice_in_dim(cross_keys, first_row_v, CAP, 0)
        cap_values = lax.dynamic_slice_in_dim(cross_values, first_row_v, CAP, 0)
        cross_scores = (
            jnp.einsum("qd,kd->qk", cross_v, cap_keys, preferred_element_type=jnp.float32)
            * score_scale
        )
        visible = cap_index[None, :] < length_v
        cross_exp = jnp.where(visible, jnp.exp(cross_scores), 0.0)
        cross_weights = (cross_exp / jnp.sum(cross_exp, axis=1, keepdims=True)).astype(jnp.bfloat16)
        cross_part = jnp.dot(cross_weights, cap_values, preferred_element_type=jnp.float32).astype(
            jnp.bfloat16
        )
        return (self_part, cross_part)

    self_parts, cross_parts = lax.map(
        attend, (query_blocks, key_blocks, value_blocks, cross_blocks, first_rows, video_lengths)
    )
    self_rows = self_parts.reshape(row_count, head_dim)
    cross_rows = cross_parts.reshape(row_count, head_dim)
    self_out, cross_out = (
        lax.all_to_all(self_rows, "seq", split_axis=0, concat_axis=1, tiled=True),
        lax.all_to_all(cross_rows, "seq", split_axis=0, concat_axis=1, tiled=True),
    )
    return (self_out, cross_out)


def solution(mesh):
    return jax.shard_map(
        per_device,
        mesh=mesh,
        in_specs=(
            P(("parts", "seq", "tp"), None),
            P(("parts", "seq", "tp"), None),
            P(("parts", "seq", "tp"), None),
            P(("parts", "seq", "tp"), None),
            P(),
            P(("parts", "seq"), "tp"),
            P("tp"),
            P("tp", None, "seq"),
            P("parts"),
            P("parts"),
        ),
        out_specs=(P(("parts", "seq", "tp"), None), P(("parts", "seq", "tp"), None)),
        check_vma=False,
    )
```

profile of v0, /device:TPU:0, one launch (start us, length us, event | category | flops | bytes accessed | tf_op | source)
XLA Modules:
  0.0 247.6 jit_solution(12408959441561960239)
XLA Ops:
  7.2 1.5 fusion.20
  8.8 2.6 %psum.14 = f32[256]{0:T(256)S(1)} all-reduce(f32[256]{0:T(256)S(1)} %fusion.20), channel_id=1, replica_groups=mesh['parts'=2,'seq'=8,'tp'=2] {'tp'}, use_global_device_ids=true, to_apply=%region_5.0 | all-reduce | flops 256 | bytes 2048 | tf_op jit(solution)/shard_map/psum | solution.py:57
  11.4 2.6 %fusion.22 = bf16[256,2048]{1,0:T(8,128)(2,1)} fusion(bf16[256,2048]{1,0:T(8,128)(2,1)} %param.17, f32[2048]{0:T(1024)} %param.18, f32[256]{0:T(256)S(1)} %add_rsqrt_fusion.1), kind=kLoop, calls=%fused_computation.32 | loop fusion | flops 2097152 | bytes 2106368 | tf_op jit(solution)/shard_map/convert_element_type | solution.py:60
  14.8 7.2 %all-to-all-start = ((bf16[128,8,128]{2,0,1:T(8,128)(2,1)}), bf16[128,8,128]{2,0,1:T(8,128)(2,1)S(1)}, u32[]{:S(2)}, u32[]{:S(2)}) async-start(bf16[128,8,128]{2,0,1:T(8,128)(2,1)} %copy_bitcast_fusion.1), calls=%async_computation | async-start | bytes 524288 | tf_op jit(solution)/shard_map/all_to_all | solution.py:44
  23.4 10.1 %all-to-all-done = bf16[128,8,128]{2,0,1:T(8,128)(2,1)S(1)} async-done(((bf16[128,8,128]{2,0,1:T(8,128)(2,1)}), bf16[128,8,128]{2,0,1:T(8,128)(2,1)S(1)}, u32[]{:S(2)}, u32[]{:S(2)}) %all-to-all-start) | async-done | bytes 262176 | tf_op jit(solution)/shard_map/all_to_all | solution.py:44
  33.5 7.2 %all-to-all-start.3 = ((bf16[128,8,128]{2,0,1:T(8,128)(2,1)}), bf16[128,8,128]{2,0,1:T(8,128)(2,1)S(1)}, u32[]{:S(2)}, u32[]{:S(2)}) async-start(bf16[128,8,128]{2,0,1:T(8,128)(2,1)} %copy_bitcast_fusion), calls=%async_computation.3 | async-start | bytes 524288 | tf_op jit(solution)/shard_map/all_to_all | solution.py:47
  40.8 108.4 %all-gather.2.cloned.1.call-done = bf16[2048,2048]{1,0:T(8,128)(2,1)} async-done(((bf16[256,2048]{1,0:T(8,128)(2,1)}), bf16[2048,2048]{1,0:T(8,128)(2,1)}) %all-gather.2.cloned.1.call-update) | async-done | bytes 8388624 | tf_op jit(solution)/shard_map/all_gather | solution.py:63
  149.2 7.1 %fusion.23 = f32[2048,256]{1,0:T(8,128)} fusion(bf16[2048,2048]{1,0:T(8,128)(2,1)} %all-gather.2.cloned.1.call-done, bf16[256,8,2,128]{3,2,1,0:T(2,128)(2,1)S(1)} %bitcast.122), kind=kOutput, calls=%fused_computation.33 | convolution fusion | flops 2147483648 | bytes 11534336 | tf_op jit(solution)/shard_map/dot_general | solution.py:62
  159.0 3.4 %all-to-all-start.1 = ((bf16[128,8,128]{0,2,1:T(8,128)(2,1)}), bf16[128,8,128]{0,2,1:T(8,128)(2,1)S(1)}, u32[]{:S(2)}, u32[]{:S(2)}) async-start(bf16[128,8,128]{0,2,1:T(8,128)(2,1)} %bitcast.4), calls=%async_computation.1 | async-start | bytes 524288 | tf_op jit(solution)/shard_map/all_to_all | solution.py:45
  162.9 8.3 %all-to-all-done.1 = bf16[128,8,128]{0,2,1:T(8,128)(2,1)S(1)} async-done(((bf16[128,8,128]{0,2,1:T(8,128)(2,1)}), bf16[128,8,128]{0,2,1:T(8,128)(2,1)S(1)}, u32[]{:S(2)}, u32[]{:S(2)}) %all-to-all-start.1) | async-done | bytes 262176 | tf_op jit(solution)/shard_map/all_to_all | solution.py:45
  171.2 3.6 %all-to-all-start.2 = ((bf16[128,8,128]{0,2,1:T(8,128)(2,1)}), bf16[128,8,128]{0,2,1:T(8,128)(2,1)S(1)}, u32[]{:S(2)}, u32[]{:S(2)}) async-start(bf16[128,8,128]{0,2,1:T(8,128)(2,1)} %bitcast.12), calls=%async_computation.2 | async-start | bytes 524288 | tf_op jit(solution)/shard_map/all_to_all | solution.py:46
  175.0 8.3 %all-to-all-done.2 = bf16[128,8,128]{0,2,1:T(8,128)(2,1)S(1)} async-done(((bf16[128,8,128]{0,2,1:T(8,128)(2,1)}), bf16[128,8,128]{0,2,1:T(8,128)(2,1)S(1)}, u32[]{:S(2)}, u32[]{:S(2)}) %all-to-all-start.2) | async-done | bytes 262176 | tf_op jit(solution)/shard_map/all_to_all | solution.py:46
  184.0 2.2 all_gather.9
  186.1 2.2 all_gather.10
  188.7 1.7 multiply_reduce_fusion
  190.4 1.3 slice.34
  192.1 22.8 %while.13 = (s32[]{:T(128)}, bf16[4,256,128]{2,1,0:T(8,128)(2,1)S(1)}, bf16[4,256,128]{2,1,0:T(8,128)(2,1)}, bf16[4,256,128]{2,1,0:T(8,128)(2,1)S(1)}, bf16[4,2,...) while((s32[]{:T(128)}, ...), condition=%wide.region_11.12_spmd.clone, body=%wide.region_8.11_spmd.clone.sunk | while | flops 135462912 | bytes 3413723 | solution.py:107
  196.2 0.9 fusion.49
  201.9 0.9 fusion.49
  207.6 0.9 fusion.49
  213.3 0.9 fusion.49
  214.9 12.6 %all_to_all.96 = bf16[8,128,128]{2,1,0:T(8,128)(2,1)S(1)} all-to-all(bf16[8,128,128]{2,1,0:T(8,128)(2,1)S(1)} %bitcast.121), channel_id=1, replica_groups=mesh['parts'=2,'seq'=8,'tp'=2] {'seq'}, dimensions={0} | all-to-all | bytes 524288 | tf_op jit(solution)/shard_map/all_to_all | solution.py:113
  227.5 3.6 %all-to-all-start.5 = ((bf16[8,128,128]{2,1,0:T(8,128)(2,1)}), bf16[8,128,128]{2,1,0:T(8,128)(2,1)S(1)}, u32[]{:S(2)}, u32[]{:S(2)}) async-start(bf16[8,128,128]{2,1,0:T(8,128)(2,1)} %bitcast.25), calls=%async_computation.5 | async-start | bytes 524288 | tf_op jit(solution)/shard_map/all_to_all | solution.py:114
  232.1 7.5 %all-to-all-done.5 = bf16[8,128,128]{2,1,0:T(8,128)(2,1)S(1)} async-done(((bf16[8,128,128]{2,1,0:T(8,128)(2,1)}), bf16[8,128,128]{2,1,0:T(8,128)(2,1)S(1)}, u32[]{:S(2)}, u32[]{:S(2)}) %all-to-all-start.5) | async-done | bytes 262176 | tf_op jit(solution)/shard_map/all_to_all | solution.py:114
  (82 shorter events, 20.2 us)
Async XLA Ops:
  7.2 6.9 %copy-start = (bf16[128,1024]{1,0:T(8,128)(2,1)S(1)}, bf16[128,1024]{1,0:T(8,128)(2,1)}, u32[]{:S(2)}) copy-start(bf16[128,1024]{1,0:T(8,128)(2,1)} %param.12) | copy-start | bytes 786436
  7.2 142.0 %all-gather.2.cloned.1.call-start = ((), (), s32[]{:S(2)}) async-start(), calls=%async_computation.6 | async-start | bytes 9437184 | tf_op jit(solution)/shard_map/all_gather | solution.py:63
  11.4 11.3 %copy-start.7 = (s32[4]{0:T(128)S(1)}, s32[4]{0:T(128)}, u32[]{:S(2)}) copy-start(s32[4]{0:T(128)} %param.21) | copy-start | bytes 52
  11.4 11.3 %copy-start.2 = (bf16[128,1024]{1,0:T(8,128)(2,1)S(1)}, bf16[128,1024]{1,0:T(8,128)(2,1)}, u32[]{:S(2)}) copy-start(bf16[128,1024]{1,0:T(8,128)(2,1)} %param.15) | copy-start | bytes 786436
  14.0 135.2 %copy-start.5 = (bf16[2048,2,128]{2,1,0:T(2,128)(2,1)S(1)}, bf16[2048,2,128]{2,1,0:T(2,128)(2,1)}, u32[]{:S(2)}) copy-start(bf16[2048,2,128]{2,1,0:T(2,128)(2,1)} %param.19) | copy-start | bytes 3145732
  14.8 18.7 %all-to-all-start = ((bf16[128,8,128]{2,0,1:T(8,128)(2,1)}), bf16[128,8,128]{2,0,1:T(8,128)(2,1)S(1)}, u32[]{:S(2)}, u32[]{:S(2)}) async-start(bf16[128,8,128]{2,0,1:T(8,128)(2,1)} %copy_bitcast_fusion.1), calls=%async_computation | async-start | bytes 524288 | tf_op jit(solution)/shard_map/all_to_all | solution.py:44
  33.5 125.5 %all-to-all-start.3 = ((bf16[128,8,128]{2,0,1:T(8,128)(2,1)}), bf16[128,8,128]{2,0,1:T(8,128)(2,1)S(1)}, u32[]{:S(2)}, u32[]{:S(2)}) async-start(bf16[128,8,128]{2,0,1:T(8,128)(2,1)} %copy_bitcast_fusion), calls=%async_computation.3 | async-start | bytes 524288 | tf_op jit(solution)/shard_map/all_to_all | solution.py:47
  40.8 147.9 %all-reduce.2.cloned.1.call-start = ((), (), s32[]{:S(2)}) async-start(), calls=%async_computation.7 | async-start | bytes 4194304 | tf_op jit(solution)/shard_map/psum | solution.py:67
  156.3 0.7 copy-start.6
  156.3 1.0 copy-start.3
  156.3 1.8 copy-start.4
  159.0 12.2 %all-to-all-start.1 = ((bf16[128,8,128]{0,2,1:T(8,128)(2,1)}), bf16[128,8,128]{0,2,1:T(8,128)(2,1)S(1)}, u32[]{:S(2)}, u32[]{:S(2)}) async-start(bf16[128,8,128]{0,2,1:T(8,128)(2,1)} %bitcast.4), calls=%async_computation.1 | async-start | bytes 524288 | tf_op jit(solution)/shard_map/all_to_all | solution.py:45
  171.2 12.2 %all-to-all-start.2 = ((bf16[128,8,128]{0,2,1:T(8,128)(2,1)}), bf16[128,8,128]{0,2,1:T(8,128)(2,1)S(1)}, u32[]{:S(2)}, u32[]{:S(2)}) async-start(bf16[128,8,128]{0,2,1:T(8,128)(2,1)} %bitcast.12), calls=%async_computation.2 | async-start | bytes 524288 | tf_op jit(solution)/shard_map/all_to_all | solution.py:46
  188.7 3.0 %copy-start.1 = (f32[2048,256]{1,0:T(8,128)S(1)}, f32[2048,256]{1,0:T(8,128)}, u32[]{:S(2)}) copy-start(f32[2048,256]{1,0:T(8,128)} %all-reduce.2.cloned.1.call-done) | copy-start | bytes 6291460
  227.5 12.2 %all-to-all-start.5 = ((bf16[8,128,128]{2,1,0:T(8,128)(2,1)}), bf16[8,128,128]{2,1,0:T(8,128)(2,1)S(1)}, u32[]{:S(2)}, u32[]{:S(2)}) async-start(bf16[8,128,128]{2,1,0:T(8,128)(2,1)} %bitcast.25), calls=%async_computation.5 | async-start | bytes 524288 | tf_op jit(solution)/shard_map/all_to_all | solution.py:114
Sparse Core Ops, SparseCore 0:
  14.2 134.9 all-gather.1
  156.5 19.3 all-reduce.1
where the time goes:
time: 249 us; the launch traced here: 248 us
  waiting for transfers between devices  143 us (57%)
  starting transfers between devices  25 us (10%)
  blocking collectives  19.5 us (8%)
  matrix products  14.7 us (6%)
  between operations  14.3 us (6%)
  local copies, waits for them, and re-layouts  13.2 us (5%)
  other arithmetic  10.2 us (4%)
  loops' own time  7.91 us (3%)
    all_gather x1, waiting for transfers between devices, per_device(): lax.all_gather(text_normed, 'seq', axis=0, tiled=True)  108 us
    all_to_all x1, blocking collectives, per_device(): lax.all_to_all(self_rows, 'seq', split_axis=0, concat_axis=1, tiled=True)  12.6 us
    all_to_all x1, waiting for transfers between devices, per_device(): lax.all_to_all(video_q, 'seq', split_axis=1, concat_axis=0, tiled=True)  10.1 us
    all_to_all x1, waiting for transfers between devices, per_device(): lax.all_to_all(video_v, 'seq', split_axis=1, concat_axis=0, tiled=True)  8.35 us
    all_to_all x1, waiting for transfers between devices, per_device(): lax.all_to_all(video_k, 'seq', split_axis=1, concat_axis=0, tiled=True)  8.28 us
    another operation x1, loops' own time, per_device(): lax.map(attend, (query_blocks, key_blocks, value_blocks, cross_blocks, fi...  7.91 us
    all_to_all x1, waiting for transfers between devices, per_device(): lax.all_to_all(cross_rows, 'seq', split_axis=0, concat_axis=1, tiled=True)  7.53 us
    all_to_all x1, starting transfers between devices, per_device(): lax.all_to_all(cross_q, 'seq', split_axis=1, concat_axis=0, tiled=True)  7.21 us
  transfers between devices with their start and end apart: 7, of which 5 were waited for; matrix products, arithmetic and copies ran while one was open for 6% of the time, Pallas kernels for 0%

commit v1 on v0

v1 whole, which is shorter than its diff:
```python
import functools
import math

import jax
import jax.numpy as jnp
from jax import lax
from jax.experimental import pallas as pl
from jax.experimental.pallas import tpu as pltpu
from jax.sharding import PartitionSpec as P

EPS = 1e-06
MESH = pl.DeviceIdType.MESH
F32, BF16 = jnp.float32, jnp.bfloat16


def head_norm(rows, gain):
    values = rows.astype(F32)
    inverse = lax.rsqrt(jnp.mean(values * values, axis=-1, keepdims=True) + EPS)
    return (values * inverse * gain).astype(BF16)


def kernel(
    dims, q_ref, k_ref, v_ref, cq_ref, gains_ref, cap_ref, tg_ref, w_ref, len_ref, vp_ref,
    self_ref, cross_ref,
    wbuf, capbuf, ssbuf, tn, pb, prb, kvs, kvbuf, sbuf, kn, sost, sob, cqbuf, qn, cost, cob,
    w_send, w_recv, f_send, cap_send, cap_recv, ss_send, ss_recv, p_send, p_recv,
    kv_send, kv_recv, kf_send, self_send, self_recv, cq_send, cq_recv,
    so_send, so_recv, co_send, co_recv, loc_sem,
):
    parts, n, T, V = dims
    gr = n // V
    G = gr * T
    p, s, c = lax.axis_index("parts"), lax.axis_index("seq"), lax.axis_index("tp")
    v, r = lax.div(s, gr), lax.rem(s, gr)
    g = r * T + c
    R, DM = q_ref.shape
    CR, FH = cap_ref.shape
    HD = DM // n
    HC = DM // G
    HL = HC // HD
    PR = FH // parts
    ROWS = gr * CR
    HR = ROWS // T
    scale = 1.0 / math.sqrt(HD)

    def mod(a, m):
        return lax.rem(a, m)

    def rc(src, dst, ss, rs, dev):
        return pltpu.make_async_remote_copy(
            src_ref=src, dst_ref=dst, send_sem=ss, recv_sem=rs, device_id=dev, device_id_type=MESH
        )

    def cols(i, width):
        return pl.ds(pl.multiple_of(i * width, width), width)

    def prow(i):
        return pl.ds(pl.multiple_of(i * PR, PR), PR)

    barrier = pltpu.get_barrier_semaphore()
    greeted = [(p, mod(s + d, n), c) for d in range(1, n)]
    greeted += [(p, v * gr + x, mod(c + d, T)) for x in range(gr) for d in range(1, T)]
    greeted += [(mod(p + d, parts), s, c) for d in range(1, parts)]
    for dev in greeted:
        pl.semaphore_signal(barrier, inc=1, device_id=dev, device_id_type=MESH)
    pl.semaphore_wait(barrier, len(greeted))

    pending = []

    def go(copy):
        copy.start()
        pending.append(copy)

    for d in range(1, V):
        go(rc(w_ref.at[prow(p)], wbuf.at[v, prow(p)], w_send.at[d], w_recv.at[v, p],
              (p, mod(v + d, V) * gr + r, c)))
    for d in range(1, gr):
        go(rc(cap_ref, capbuf.at[r], cap_send.at[d], cap_recv.at[r],
              (p, v * gr + mod(r + d, gr), c)))
    own = []
    for a, ref in enumerate((q_ref, k_ref, v_ref)):
        for d in range(1, G):
            gg = mod(g + d, G)
            go(rc(ref.at[:, cols(gg, HC)], sbuf.at[a, g], self_send.at[a, d], self_recv.at[a, g],
                  (p, v * gr + lax.div(gg, T), mod(gg, T))))
        own.append(pltpu.make_async_copy(ref.at[:, cols(g, HC)], sbuf.at[a, g], loc_sem.at[a]))
    own.append(pltpu.make_async_copy(cq_ref.at[:, cols(s, HD)], cqbuf.at[s], loc_sem.at[3]))
    for copy in own:
        copy.start()
    for d in range(1, n):
        t = mod(s + d, n)
        go(rc(cq_ref.at[:, cols(t, HD)], cqbuf.at[s], cq_send.at[d], cq_recv.at[s], (p, t, c)))

    def wait_in(dst, sem):
        rc(dst, dst, loc_sem.at[4], sem, (p, mod(s + 1, n), c)).wait_recv()

    CH = 16

    def squares(src, row0):
        def step(i, carry):
            x = src[pl.ds(pl.multiple_of(i * CH, CH), CH), :].astype(F32)
            total = jnp.sum(x * x, axis=1, keepdims=True)
            ssbuf[c, pl.ds(pl.multiple_of(row0 + i * CH, CH), CH), :] = jnp.broadcast_to(total, (CH, 128))
            return carry
        lax.fori_loop(0, CR // CH, step, 0)

    def normalize(src, row0):
        def step(i, carry):
            x = src[pl.ds(pl.multiple_of(i * CH, CH), CH), :].astype(F32)
            rows = pl.ds(pl.multiple_of(row0 + i * CH, CH), CH)
            total = ssbuf[0, rows, :]
            for t in range(1, T):
                total = total + ssbuf[t, rows, :]
            inverse = lax.rsqrt(total[:, :1] / (FH * T) + EPS)
            tn[rows, :] = (x * inverse * tg_ref[...]).astype(BF16)
            return carry
        lax.fori_loop(0, CR // CH, step, 0)

    squares(cap_ref, r * CR)
    for d in range(1, gr):
        rr = mod(r + d, gr)
        wait_in(capbuf.at[rr], cap_recv.at[rr])
        squares(capbuf.at[rr], rr * CR)
    for d in range(1, T):
        go(rc(ssbuf.at[c], ssbuf.at[c], ss_send.at[d], ss_recv.at[c], (p, s, mod(c + d, T))))

    for copy in own:
        copy.wait()
    for a in (1, 0, 2):
        for d in range(1, G):
            gg = mod(g + d, G)
            wait_in(sbuf.at[a, gg], self_recv.at[a, gg])
    for j in range(HL):
        js = slice(j * HD, (j + 1) * HD)
        gain = gains_ref[1:2, cols(g * HL + j, HD)]

        def knorm(i, carry):
            kn[i, :, js] = head_norm(sbuf[1, i, :, js], gain)
            return carry
        lax.fori_loop(0, G, knorm, 0)

    def attend_self(gg):
        for j in range(HL):
            js = slice(j * HD, (j + 1) * HD)
            gain = gains_ref[0:1, cols(g * HL + j, HD)]
            queries = head_norm(sbuf[0, gg, :, js], gain)
            keys = kn[:, :, js].reshape(G * R, HD)
            scores = lax.dot_general(queries, keys, (((1,), (1,)), ((), ())),
                                     preferred_element_type=F32)
            e = jnp.exp(scores * scale)
            total = jnp.sum(e, axis=1, keepdims=True)
            values = sbuf[2, :, :, js].reshape(G * R, HD)
            o = jnp.dot(e.astype(BF16), values, preferred_element_type=F32) / total
            sost[gg, :, js] = o.astype(BF16)

    def self_step(i, carry):
        gg = mod(g + 1 + i, G)
        attend_self(gg)
        rc(sost.at[gg], sob.at[:, cols(g, HC)], so_send.at[gg], so_recv.at[g],
           (p, v * gr + lax.div(gg, T), mod(gg, T))).start()
        return carry
    lax.fori_loop(0, G - 1, self_step, 0)
    attend_self(g)
    sob[:, cols(g, HC)] = sost[g]

    for d in range(1, V):
        vv = mod(v + d, V)
        wait_in(wbuf.at[vv, prow(p)], w_recv.at[vv, p])
        for e in range(1, parts):
            go(rc(wbuf.at[vv, prow(p)], wbuf.at[vv, prow(p)], f_send.at[d, e], w_recv.at[vv, p],
                  (mod(p + e, parts), s, c)))

    for d in range(1, T):
        cc = mod(c + d, T)
        wait_in(ssbuf.at[cc], ss_recv.at[cc])
    normalize(cap_ref, r * CR)
    for d in range(1, gr):
        rr = mod(r + d, gr)
        normalize(capbuf.at[rr], rr * CR)

    for d in range(1, n):
        t = mod(s + d, n)
        wait_in(cqbuf.at[t], cq_recv.at[t])
    cross_gain = gains_ref[2:3, cols(s, HD)]

    def qnorm(i, carry):
        qn[i] = head_norm(cqbuf[i], cross_gain)
        return carry
    lax.fori_loop(0, n, qnorm, 0)

    for d in range(V):
        vv = mod(v + d, V)
        if d == 0:
            weight = w_ref[...]
        else:
            for e in range(1, parts):
                pp = mod(p + e, parts)
                wait_in(wbuf.at[vv, prow(pp)], w_recv.at[vv, pp])
            weight = wbuf[vv]
        for e in range(1, T + 1):
            cc = mod(c + e, T)
            rows = pl.ds(pl.multiple_of(cc * HR, HR), HR)
            pb[d, cc] = jnp.dot(tn[rows, :], weight, preferred_element_type=F32)
            if e < T:
                go(rc(pb.at[d, cc], prb.at[d, c], p_send.at[d, e], p_recv.at[d, c], (p, s, cc)))
        total = pb[d, c]
        for e in range(1, T):
            cc = mod(c + e, T)
            wait_in(prb.at[d, cc], p_recv.at[d, cc])
            total = total + prb[d, cc]
        gain = gains_ref[3:4, cols(vv * gr + r, HD)]
        keys = head_norm(total[:, :HD], gain)
        values = total[:, HD:].astype(BF16)
        if d == 0:
            kvbuf[v, c, :, :HD] = keys
            kvbuf[v, c, :, HD:] = values
            for e in range(1, T):
                go(rc(kvbuf.at[v, c], kvbuf.at[v, c], kf_send.at[d, e], kv_recv.at[v, c],
                      (p, s, mod(c + e, T))))
        else:
            kvs[d, :, :HD] = keys
            kvs[d, :, HD:] = values
            go(rc(kvs.at[d], kvbuf.at[v, c], kv_send.at[d], kv_recv.at[v, c],
                  (p, vv * gr + r, c)))
    for d in range(1, V):
        vv = mod(v + V - d, V)
        wait_in(kvbuf.at[vv, c], kv_recv.at[vv, c])
        for e in range(1, T):
            go(rc(kvbuf.at[vv, c], kvbuf.at[vv, c], kf_send.at[d, e], kv_recv.at[vv, c],
                  (p, s, mod(c + e, T))))
    for d in range(V):
        vv = mod(v + V - d, V)
        for e in range(1, T):
            cc = mod(c + e, T)
            wait_in(kvbuf.at[vv, cc], kv_recv.at[vv, cc])

    def attend_cross(vv):
        prompt = vp_ref[vv]
        length = len_ref[prompt]
        kv = kvbuf[prompt].reshape(ROWS, 2 * HD)
        queries = qn[pl.ds(vv * gr, gr)].reshape(gr * R, HD)
        scores = lax.dot_general(queries, kv[:, :HD], (((1,), (1,)), ((), ())),
                                 preferred_element_type=F32)
        visible = lax.broadcasted_iota(jnp.int32, (1, ROWS), 1) < length
        e = jnp.where(visible, jnp.exp(scores * scale), 0.0)
        total = jnp.sum(e, axis=1, keepdims=True)
        o = jnp.dot(e.astype(BF16), kv[:, HD:], preferred_element_type=F32) / total
        cost[pl.ds(vv * gr, gr)] = o.astype(BF16).reshape(gr, R, HD)

    def co_copy(t):
        return rc(cost.at[t], cob.at[:, cols(s, HD)], co_send.at[t], co_recv.at[s], (p, t, c))

    def cross_step(i, carry):
        vv = mod(v + 1 + i, V)
        attend_cross(vv)
        for x in range(gr):
            co_copy(vv * gr + x).start()
        return carry
    lax.fori_loop(0, V - 1, cross_step, 0)
    attend_cross(v)
    for d in range(1, gr):
        co_copy(v * gr + mod(r + d, gr)).start()
    cob[:, cols(s, HD)] = cost[s]

    for d in range(1, G):
        gg = mod(g + d, G)
        wait_in(sob.at[:, cols(gg, HC)], so_recv.at[gg])
    self_ref[...] = sob[...]
    for d in range(1, n):
        t = mod(s + d, n)
        wait_in(cob.at[:, cols(t, HD)], co_recv.at[t])
    cross_ref[...] = cob[...]

    for copy in pending:
        copy.wait_send()
    for d in range(1, G):
        gg = mod(g + d, G)
        rc(sost.at[gg], sob.at[:, cols(g, HC)], so_send.at[gg], so_recv.at[g],
           (p, v * gr + lax.div(gg, T), mod(gg, T))).wait_send()
    for d in range(1, n):
        co_copy(mod(s + d, n)).wait_send()


def per_device(
    video_q, video_k, video_v, cross_q, qk_gains, captions, text_gain, cross_kv_weight,
    lengths, video_prompt,
):
    parts, n, T = (lax.axis_size(a) for a in ("parts", "seq", "tp"))
    V = lengths.shape[0]
    gr = n // V
    G = gr * T
    R, DM = video_q.shape
    CR, FH = captions.shape
    HD = DM // n
    HC = DM // G
    ROWS = gr * CR
    HR = ROWS // T
    weight = cross_kv_weight.reshape(FH, 2 * HD)
    vm = pl.BlockSpec(memory_space=pltpu.VMEM)
    sm = pl.BlockSpec(memory_space=pltpu.SMEM)
    sem = pltpu.SemaphoreType.DMA
    VM = pltpu.VMEM
    return pl.pallas_call(
        functools.partial(kernel, (parts, n, T, V)),
        out_shape=(
            jax.ShapeDtypeStruct((R, DM), BF16),
            jax.ShapeDtypeStruct((R, DM), BF16),
        ),
        in_specs=[vm] * 8 + [sm] * 2,
        out_specs=(vm, vm),
        scratch_shapes=[
            VM((V, FH, 2 * HD), BF16),
            VM((gr, CR, FH), BF16),
            VM((T, ROWS, 128), F32),
            VM((ROWS, FH), BF16),
            VM((V, T, HR, 2 * HD), F32),
            VM((V, T, HR, 2 * HD), F32),
            VM((V, HR, 2 * HD), BF16),
            VM((V, T, HR, 2 * HD), BF16),
            VM((3, G, R, HC), BF16),
            VM((G, R, HC), BF16),
            VM((G, R, HC), BF16),
            VM((R, DM), BF16),
            VM((n, R, HD), BF16),
            VM((n, R, HD), BF16),
            VM((n, R, HD), BF16),
            VM((R, DM), BF16),
            sem((V,)), sem((V, parts)), sem((V, parts)),
            sem((gr,)), sem((gr,)),
            sem((T,)), sem((T,)),
            sem((V, T)), sem((V, T)),
            sem((V,)), sem((V, T)), sem((V, T)),
            sem((3, G)), sem((3, G)),
            sem((n,)), sem((n,)),
            sem((G,)), sem((G,)),
            sem((n,)), sem((n,)),
            sem((5,)),
        ],
        compiler_params=pltpu.CompilerParams(
            collective_id=0, has_side_effects=True, vmem_limit_bytes=56 * 1024 * 1024
        ),
    )(
        video_q, video_k, video_v, cross_q, qk_gains, captions, text_gain.reshape(1, FH), weight,
        lengths, video_prompt,
    )


def solution(mesh):
    rows = P(("parts", "seq", "tp"), None)
    return jax.shard_map(
        per_device,
        mesh=mesh,
        in_specs=(
            rows, rows, rows, rows, P(), P(("parts", "seq"), "tp"), P("tp"),
            P("tp", None, "seq"), P("parts"), P("parts"),
        ),
        out_specs=(rows, rows),
        check_vma=False,
    )
```

time: 249 us -> 113 us (0.45)
  waiting for transfers between devices: 143 us -> 0 us
  Pallas kernels: 0 us -> 107 us
  starting transfers between devices: 25 us -> 0 us
  blocking collectives: 19.5 us -> 0 us
  matrix products: 14.7 us -> 0 us
  between operations: 14.3 us -> 0.65 us
  other arithmetic: 10.2 us -> 0 us
  local copies, waits for them, and re-layouts: 13.2 us -> 4.76 us
  loops' own time: 7.91 us -> 0 us
    all_gather x1 -> x0, waiting for transfers between devices: 108 us -> none  [per_device(): lax.all_gather(text_normed, 'seq', axis=0, tiled=True)]
    pallas_call x0 -> x1, Pallas kernels: none -> 107 us  [per_device(): pl.pallas_call(functools.partial(kernel, (parts, n, T, V)), out_shape=(ja...]
    all_to_all x5 -> x0, waiting for transfers between devices: 34.3 us -> none  [the longest x1 10.1 us: per_device(): lax.all_to_all(video_q, 'seq', split_axis=1, concat_axis=0, tiled=True)]
    all_to_all x5 -> x0, starting transfers between devices: 24.9 us -> none  [the longest x1 7.21 us: per_device(): lax.all_to_all(cross_q, 'seq', split_axis=1, concat_axis=0, tiled=True)]
    dot_general x17 -> x0, matrix products: 14.7 us -> none  [the longest x1 7.14 us: per_device(): jnp.dot(lax.all_gather(text_normed, 'seq', axis=0, tiled=True), weight, p...]
    all_to_all x1 -> x0, blocking collectives: 12.6 us -> none  [per_device(): lax.all_to_all(self_rows, 'seq', split_axis=0, concat_axis=1, tiled=True)]
    another operation x1 -> x0, loops' own time: 7.91 us -> none  [per_device(): lax.map(attend, (query_blocks, key_blocks, value_blocks, cross_blocks, fi...]
    dynamic_slice x13 -> x0, local copies, waits for them, and re-layouts: 5.45 us -> none  [the longest x12 4.77 us: per_device(): lax.map(attend, (query_blocks, key_blocks, value_blocks, cross_blocks, fi...]
  transfers between devices with their start and end apart: 7 -> 0, of which waited for: 5 -> 0; matrix products, arithmetic and copies ran while one was open for 6% -> 0% of each run, Pallas kernels for 0% -> 0%
where the time goes in v1:
time: 113 us
  Pallas kernels  107 us (95%)
  local copies, waits for them, and re-layouts  4.76 us (4%)
    pallas_call x1, Pallas kernels, per_device(): pl.pallas_call(functools.partial(kernel, (parts, n, T, V)), out_shape=(ja...  107 us
    unnamed x5, local copies, waits for them, and re-layouts  4.76 us

profile of v1, /device:TPU:0, one launch (start us, length us, event | category | flops | bytes accessed | tf_op | source)
XLA Modules:
  0.0 112.9 jit_solution(5769299819906176915)
XLA Ops:
  0.6 2.3 %copy.14 = bf16[256,8,2,128]{3,1,2,0:T(8,128)(2,1)} copy(bf16[256,8,2,128]{3,2,1,0:T(2,128)(2,1)} %bitcast.6) | data formatting | bytes 2097152
  3.0 107.5 %shard_map.113 = (bf16[128,1024]{1,0:T(8,128)(2,1)}, bf16[128,1024]{1,0:T(8,128)(2,1)}) custom-call(bf16[128,1024]{1,0:T(8,128)(2,1)} %q_ref.1, bf16[128,1024]{1,0:T(8,128)(2,1)} %k_ref.1, bf16[128,1024]{1,0:T(8,128)(2,1)} %v_ref.1, bf16[128,1024]{1,0:T(8,128)(2,1)} %cq_ref.1, f32[4,1024]{1,0:T(4,128)} %gains_ref.1, bf16[256,2048]{1,0:T(8,128)(2,1)} %cap_ref.1, ...), custom_call_target="tpu_custom_call" | custom-call | tf_op jit(solution)/shard_map/pallas_call | solution.py:303
  110.5 0.0 copy-start
  110.5 1.7 %copy.17 = bf16[128,1024]{1,0:T(8,128)(2,1)} copy(bf16[128,1024]{1,0:T(8,128)(2,1)} %get-tuple-element.4) | data formatting | bytes 524288
  112.2 0.0 copy-done
  112.2 0.7 copy.18
Async XLA Ops:
  110.5 1.7 %copy-start = (bf16[128,1024]{1,0:T(8,128)(2,1)S(1)}, bf16[128,1024]{1,0:T(8,128)(2,1)}, u32[]{:S(2)}) copy-start(bf16[128,1024]{1,0:T(8,128)(2,1)} %get-tuple-element.5) | copy-start | bytes 786436

commit v2 on v1

--- a/solution.py
+++ b/solution.py
@@ -11,6 +11,7 @@
 EPS = 1e-06
 MESH = pl.DeviceIdType.MESH
 F32, BF16 = jnp.float32, jnp.bfloat16
+Q = 2
 
 
 def head_norm(rows, gain):
@@ -23,7 +24,7 @@
     dims, q_ref, k_ref, v_ref, cq_ref, gains_ref, cap_ref, tg_ref, w_ref, len_ref, vp_ref,
     self_ref, cross_ref,
     wbuf, capbuf, ssbuf, tn, pb, prb, kvs, kvbuf, sbuf, kn, sost, sob, cqbuf, qn, cost, cob,
-    w_send, w_recv, f_send, cap_send, cap_recv, ss_send, ss_recv, p_send, p_recv,
+    wr_send, wl_send, w_recv, f_send, cap_send, cap_recv, ss_send, ss_recv, p_send, p_recv,
     kv_send, kv_recv, kf_send, self_send, self_recv, cq_send, cq_recv,
     so_send, so_recv, co_send, co_recv, loc_sem,
 ):
@@ -38,7 +39,7 @@
     HD = DM // n
     HC = DM // G
     HL = HC // HD
-    PR = FH // parts
+    PR = FH // (parts * Q)
     ROWS = gr * CR
     HR = ROWS // T
     scale = 1.0 / math.sqrt(HD)
@@ -54,8 +55,20 @@
     def cols(i, width):
         return pl.ds(pl.multiple_of(i * width, width), width)
 
-    def prow(i):
-        return pl.ds(pl.multiple_of(i * PR, PR), PR)
+    def prow(i, q):
+        return pl.ds(pl.multiple_of((i * Q + q) * PR, PR), PR)
+
+    left_of, right_of = v, V - 1 - v
+    both = jnp.minimum(left_of, right_of)
+
+    def nearest(k):
+        near = k // 2 + 1
+        far = k - both + 1
+        return jnp.where(
+            k < 2 * both,
+            v - near if k % 2 == 0 else v + near,
+            jnp.where(left_of > right_of, v - far, v + far),
+        )
 
     barrier = pltpu.get_barrier_semaphore()
     greeted = [(p, mod(s + d, n), c) for d in range(1, n)]
@@ -67,33 +80,46 @@
 
     pending = []
 
-    def go(copy):
-        copy.start()
-        pending.append(copy)
-
-    for d in range(1, V):
-        go(rc(w_ref.at[prow(p)], wbuf.at[v, prow(p)], w_send.at[d], w_recv.at[v, p],
-              (p, mod(v + d, V) * gr + r, c)))
+    def go(copy, when=None):
+        pending.append((copy, when))
+        if when is None:
+            copy.start()
+        else:
+            pl.when(when)(copy.start)
+
+    def wait_in(dst, sem):
+        rc(dst, dst, loc_sem.at[4], sem, (p, mod(s + 1, n), c)).wait_recv()
+
+    def pass_on(src, u, q, step, when):
+        row = prow(p, q)
+        target = jnp.clip(v + step, 0, V - 1) * gr + r
+        sems = wr_send if step > 0 else wl_send
+        go(rc(src, wbuf.at[u, row], sems.at[u, q], w_recv.at[u, p, q], (p, target, c)), when)
+
+    for q in range(Q):
+        pass_on(w_ref.at[prow(p, q)], v, q, 1, v + 1 < V)
+        pass_on(w_ref.at[prow(p, q)], v, q, -1, v > 0)
+
+    def weight_step(d):
+        for q in range(Q):
+            row = prow(p, q)
+            for step in (1, -1):
+                there = v - step * d
+                here = (there >= 0) & (there < V)
+                u = jnp.clip(there, 0, V - 1)
+
+                @pl.when(here)
+                def _():
+                    wait_in(wbuf.at[u, row], w_recv.at[u, p, q])
+                onward = here & ((v + step >= 0) & (v + step < V))
+                pass_on(wbuf.at[u, row], u, q, step, onward)
+                for e in range(1, parts):
+                    go(rc(wbuf.at[u, row], wbuf.at[u, row], f_send.at[u, e, q],
+                          w_recv.at[u, p, q], (mod(p + e, parts), s, c)), here)
+
     for d in range(1, gr):
         go(rc(cap_ref, capbuf.at[r], cap_send.at[d], cap_recv.at[r],
               (p, v * gr + mod(r + d, gr), c)))
-    own = []
-    for a, ref in enumerate((q_ref, k_ref, v_ref)):
-        for d in range(1, G):
-            gg = mod(g + d, G)
-            go(rc(ref.at[:, cols(gg, HC)], sbuf.at[a, g], self_send.at[a, d], self_recv.at[a, g],
-                  (p, v * gr + lax.div(gg, T), mod(gg, T))))
-        own.append(pltpu.make_async_copy(ref.at[:, cols(g, HC)], sbuf.at[a, g], loc_sem.at[a]))
-    own.append(pltpu.make_async_copy(cq_ref.at[:, cols(s, HD)], cqbuf.at[s], loc_sem.at[3]))
-    for copy in own:
-        copy.start()
-    for d in range(1, n):
-        t = mod(s + d, n)
-        go(rc(cq_ref.at[:, cols(t, HD)], cqbuf.at[s], cq_send.at[d], cq_recv.at[s], (p, t, c)))
-
-    def wait_in(dst, sem):
-        rc(dst, dst, loc_sem.at[4], sem, (p, mod(s + 1, n), c)).wait_recv()
-
     CH = 16
 
     def squares(src, row0):
@@ -117,59 +143,28 @@
         lax.fori_loop(0, CR // CH, step, 0)
 
     squares(cap_ref, r * CR)
+    weight_step(1)
+    for d in range(1, n):
+        t = mod(s + d, n)
+        go(rc(cq_ref.at[:, cols(t, HD)], cqbuf.at[s], cq_send.at[d], cq_recv.at[s], (p, t, c)))
+    for d in range(2, V - 1):
+        weight_step(d)
     for d in range(1, gr):
         rr = mod(r + d, gr)
         wait_in(capbuf.at[rr], cap_recv.at[rr])
         squares(capbuf.at[rr], rr * CR)
     for d in range(1, T):
         go(rc(ssbuf.at[c], ssbuf.at[c], ss_send.at[d], ss_recv.at[c], (p, s, mod(c + d, T))))
-
-    for copy in own:
-        copy.wait()
-    for a in (1, 0, 2):
+    own = []
+    for a, ref in enumerate((q_ref, k_ref, v_ref)):
         for d in range(1, G):
             gg = mod(g + d, G)
-            wait_in(sbuf.at[a, gg], self_recv.at[a, gg])
-    for j in range(HL):
-        js = slice(j * HD, (j + 1) * HD)
-        gain = gains_ref[1:2, cols(g * HL + j, HD)]
-
-        def knorm(i, carry):
-            kn[i, :, js] = head_norm(sbuf[1, i, :, js], gain)
-            return carry
-        lax.fori_loop(0, G, knorm, 0)
-
-    def attend_self(gg):
-        for j in range(HL):
-            js = slice(j * HD, (j + 1) * HD)
-            gain = gains_ref[0:1, cols(g * HL + j, HD)]
-            queries = head_norm(sbuf[0, gg, :, js], gain)
-            keys = kn[:, :, js].reshape(G * R, HD)
-            scores = lax.dot_general(queries, keys, (((1,), (1,)), ((), ())),
-                                     preferred_element_type=F32)
-            e = jnp.exp(scores * scale)
-            total = jnp.sum(e, axis=1, keepdims=True)
-            values = sbuf[2, :, :, js].reshape(G * R, HD)
-            o = jnp.dot(e.astype(BF16), values, preferred_element_type=F32) / total
-            sost[gg, :, js] = o.astype(BF16)
-
-    def self_step(i, carry):
-        gg = mod(g + 1 + i, G)
-        attend_self(gg)
-        rc(sost.at[gg], sob.at[:, cols(g, HC)], so_send.at[gg], so_recv.at[g],
-           (p, v * gr + lax.div(gg, T), mod(gg, T))).start()
-        return carry
-    lax.fori_loop(0, G - 1, self_step, 0)
-    attend_self(g)
-    sob[:, cols(g, HC)] = sost[g]
-
-    for d in range(1, V):
-        vv = mod(v + d, V)
-        wait_in(wbuf.at[vv, prow(p)], w_recv.at[vv, p])
-        for e in range(1, parts):
-            go(rc(wbuf.at[vv, prow(p)], wbuf.at[vv, prow(p)], f_send.at[d, e], w_recv.at[vv, p],
-                  (mod(p + e, parts), s, c)))
-
+            go(rc(ref.at[:, cols(gg, HC)], sbuf.at[a, g], self_send.at[a, d], self_recv.at[a, g],
+                  (p, v * gr + lax.div(gg, T), mod(gg, T))))
+        own.append(pltpu.make_async_copy(ref.at[:, cols(g, HC)], sbuf.at[a, g], loc_sem.at[a]))
+    own.append(pltpu.make_async_copy(cq_ref.at[:, cols(s, HD)], cqbuf.at[s], loc_sem.at[3]))
+    for copy in own:
+        copy.start()
     for d in range(1, T):
         cc = mod(c + d, T)
         wait_in(ssbuf.at[cc], ss_recv.at[cc])
@@ -178,24 +173,15 @@
         rr = mod(r + d, gr)
         normalize(capbuf.at[rr], rr * CR)
 
-    for d in range(1, n):
-        t = mod(s + d, n)
-        wait_in(cqbuf.at[t], cq_recv.at[t])
-    cross_gain = gains_ref[2:3, cols(s, HD)]
-
-    def qnorm(i, carry):
-        qn[i] = head_norm(cqbuf[i], cross_gain)
-        return carry
-    lax.fori_loop(0, n, qnorm, 0)
-
-    for d in range(V):
-        vv = mod(v + d, V)
+    def key_value_block(d):
+        vv = v if d == 0 else nearest(d - 1)
         if d == 0:
             weight = w_ref[...]
         else:
             for e in range(1, parts):
                 pp = mod(p + e, parts)
-                wait_in(wbuf.at[vv, prow(pp)], w_recv.at[vv, pp])
+                for q in range(Q):
+                    wait_in(wbuf.at[vv, prow(pp, q)], w_recv.at[vv, pp, q])
             weight = wbuf[vv]
         for e in range(1, T + 1):
             cc = mod(c + e, T)
@@ -222,8 +208,62 @@
             kvs[d, :, HD:] = values
             go(rc(kvs.at[d], kvbuf.at[v, c], kv_send.at[d], kv_recv.at[v, c],
                   (p, vv * gr + r, c)))
+    weight_step(V - 1)
+    key_value_block(0)
+
+    for copy in own:
+        copy.wait()
+    for a in (1, 0, 2):
+        for d in range(1, G):
+            gg = mod(g + d, G)
+            wait_in(sbuf.at[a, gg], self_recv.at[a, gg])
+    for j in range(HL):
+        js = slice(j * HD, (j + 1) * HD)
+        gain = gains_ref[1:2, cols(g * HL + j, HD)]
+
+        def knorm(i, carry):
+            kn[i, :, js] = head_norm(sbuf[1, i, :, js], gain)
+            return carry
+        lax.fori_loop(0, G, knorm, 0)
+
+    def attend_self(gg):
+        for j in range(HL):
+            js = slice(j * HD, (j + 1) * HD)
+            gain = gains_ref[0:1, cols(g * HL + j, HD)]
+            queries = head_norm(sbuf[0, gg, :, js], gain)
+            keys = kn[:, :, js].reshape(G * R, HD)
+            scores = lax.dot_general(queries, keys, (((1,), (1,)), ((), ())),
+                                     preferred_element_type=F32)
+            e = jnp.exp(scores * scale)
+            total = jnp.sum(e, axis=1, keepdims=True)
+            values = sbuf[2, :, :, js].reshape(G * R, HD)
+            o = jnp.dot(e.astype(BF16), values, preferred_element_type=F32) / total
+            sost[gg, :, js] = o.astype(BF16)
+
+    def self_step(i, carry):
+        gg = mod(g + 1 + i, G)
+        attend_self(gg)
+        rc(sost.at[gg], sob.at[:, cols(g, HC)], so_send.at[gg], so_recv.at[g],
+           (p, v * gr + lax.div(gg, T), mod(gg, T))).start()
+        return carry
+    lax.fori_loop(0, G - 1, self_step, 0)
+    attend_self(g)
+    sob[:, cols(g, HC)] = sost[g]
+
+    for d in range(1, n):
+        t = mod(s + d, n)
+        wait_in(cqbuf.at[t], cq_recv.at[t])
+    cross_gain = gains_ref[2:3, cols(s, HD)]
+
+    def qnorm(i, carry):
+        qn[i] = head_norm(cqbuf[i], cross_gain)
+        return carry
+    lax.fori_loop(0, n, qnorm, 0)
+
     for d in range(1, V):
-        vv = mod(v + V - d, V)
+        key_value_block(d)
+    for d in range(1, V):
+        vv = nearest(d - 1)
         wait_in(kvbuf.at[vv, c], kv_recv.at[vv, c])
         for e in range(1, T):
             go(rc(kvbuf.at[vv, c], kvbuf.at[vv, c], kf_send.at[d, e], kv_recv.at[vv, c],
@@ -271,8 +311,11 @@
         wait_in(cob.at[:, cols(t, HD)], co_recv.at[t])
     cross_ref[...] = cob[...]
 
-    for copy in pending:
-        copy.wait_send()
+    for copy, when in pending:
+        if when is None:
+            copy.wait_send()
+        else:
+            pl.when(when)(copy.wait_send)
     for d in range(1, G):
         gg = mod(g + d, G)
         rc(sost.at[gg], sob.at[:, cols(g, HC)], so_send.at[gg], so_recv.at[g],
@@ -325,7 +368,7 @@
             VM((n, R, HD), BF16),
             VM((n, R, HD), BF16),
             VM((R, DM), BF16),
-            sem((V,)), sem((V, parts)), sem((V, parts)),
+            sem((V, Q)), sem((V, Q)), sem((V, parts, Q)), sem((V, parts, Q)),
             sem((gr,)), sem((gr,)),
             sem((T,)), sem((T,)),
             sem((V, T)), sem((V, T)),

time: 113 us -> 80.6 us (0.71)
  Pallas kernels: 107 us -> 75 us
    pallas_call x1, Pallas kernels: 107 us -> 75 us  [per_device(): pl.pallas_call(functools.partial(kernel, (parts, n, T, V)), out_shape=(ja...]
where the time goes in v2:
time: 80.6 us; the launch traced here: 80.5 us
  Pallas kernels  75 us (93%)
  local copies, waits for them, and re-layouts  4.76 us (6%)
    pallas_call x1, Pallas kernels, per_device(): pl.pallas_call(functools.partial(kernel, (parts, n, T, V)), out_shape=(ja...  75 us
    unnamed x5, local copies, waits for them, and re-layouts  4.76 us

profile of v2, /device:TPU:0, one launch (start us, length us, event | category | flops | bytes accessed | tf_op | source)
XLA Modules:
  0.0 80.5 jit_solution(552276451641072868)
XLA Ops:
  0.6 2.3 %copy.14 = bf16[256,8,2,128]{3,1,2,0:T(8,128)(2,1)} copy(bf16[256,8,2,128]{3,2,1,0:T(2,128)(2,1)} %bitcast.6) | data formatting | bytes 2097152
  3.0 75.0 %shard_map.113 = (bf16[128,1024]{1,0:T(8,128)(2,1)}, bf16[128,1024]{1,0:T(8,128)(2,1)}) custom-call(bf16[128,1024]{1,0:T(8,128)(2,1)} %q_ref.1, bf16[128,1024]{1,0:T(8,128)(2,1)} %k_ref.1, bf16[128,1024]{1,0:T(8,128)(2,1)} %v_ref.1, bf16[128,1024]{1,0:T(8,128)(2,1)} %cq_ref.1, f32[4,1024]{1,0:T(4,128)} %gains_ref.1, bf16[256,2048]{1,0:T(8,128)(2,1)} %cap_ref.1, ...), custom_call_target="tpu_custom_call" | custom-call | tf_op jit(solution)/shard_map/pallas_call | solution.py:346
  78.0 0.0 copy-start
  78.0 1.7 %copy.17 = bf16[128,1024]{1,0:T(8,128)(2,1)} copy(bf16[128,1024]{1,0:T(8,128)(2,1)} %get-tuple-element.4) | data formatting | bytes 524288
  79.7 0.0 copy-done
  79.7 0.7 copy.18
Async XLA Ops:
  78.0 1.7 %copy-start = (bf16[128,1024]{1,0:T(8,128)(2,1)S(1)}, bf16[128,1024]{1,0:T(8,128)(2,1)}, u32[]{:S(2)}) copy-start(bf16[128,1024]{1,0:T(8,128)(2,1)} %get-tuple-element.5) | copy-start | bytes 786436

commit v3 on v2

--- a/solution.py
+++ b/solution.py
@@ -76,6 +76,10 @@
     greeted += [(mod(p + d, parts), s, c) for d in range(1, parts)]
     for dev in greeted:
         pl.semaphore_signal(barrier, inc=1, device_id=dev, device_id_type=MESH)
+    own_weight = pltpu.make_async_copy(w_ref, wbuf.at[v], loc_sem.at[5])
+    own_caption = pltpu.make_async_copy(cap_ref, capbuf.at[r], loc_sem.at[6])
+    own_caption.start()
+    own_weight.start()
     pl.semaphore_wait(barrier, len(greeted))
 
     pending = []
@@ -100,8 +104,8 @@
         pass_on(w_ref.at[prow(p, q)], v, q, 1, v + 1 < V)
         pass_on(w_ref.at[prow(p, q)], v, q, -1, v > 0)
 
-    def weight_step(d):
-        for q in range(Q):
+    def weight_step(d, pieces=range(Q)):
+        for q in pieces:
             row = prow(p, q)
             for step in (1, -1):
                 there = v - step * d
@@ -128,7 +132,7 @@
             total = jnp.sum(x * x, axis=1, keepdims=True)
             ssbuf[c, pl.ds(pl.multiple_of(row0 + i * CH, CH), CH), :] = jnp.broadcast_to(total, (CH, 128))
             return carry
-        lax.fori_loop(0, CR // CH, step, 0)
+        lax.fori_loop(0, CR // CH, step, 0, unroll=4)
 
     def normalize(src, row0):
         def step(i, carry):
@@ -140,9 +144,10 @@
             inverse = lax.rsqrt(total[:, :1] / (FH * T) + EPS)
             tn[rows, :] = (x * inverse * tg_ref[...]).astype(BF16)
             return carry
-        lax.fori_loop(0, CR // CH, step, 0)
-
-    squares(cap_ref, r * CR)
+        lax.fori_loop(0, CR // CH, step, 0, unroll=4)
+
+    own_caption.wait()
+    squares(capbuf.at[r], r * CR)
     weight_step(1)
     for d in range(1, n):
         t = mod(s + d, n)
@@ -168,7 +173,9 @@
     for d in range(1, T):
         cc = mod(c + d, T)
         wait_in(ssbuf.at[cc], ss_recv.at[cc])
-    normalize(cap_ref, r * CR)
+    weight_step(V - 1, range(Q // 2))
+    normalize(capbuf.at[r], r * CR)
+    weight_step(V - 1, range(Q // 2, Q))
     for d in range(1, gr):
         rr = mod(r + d, gr)
         normalize(capbuf.at[rr], rr * CR)
@@ -176,13 +183,13 @@
     def key_value_block(d):
         vv = v if d == 0 else nearest(d - 1)
         if d == 0:
-            weight = w_ref[...]
+            own_weight.wait()
         else:
             for e in range(1, parts):
                 pp = mod(p + e, parts)
                 for q in range(Q):
                     wait_in(wbuf.at[vv, prow(pp, q)], w_recv.at[vv, pp, q])
-            weight = wbuf[vv]
+        weight = wbuf[vv]
         for e in range(1, T + 1):
             cc = mod(c + e, T)
             rows = pl.ds(pl.multiple_of(cc * HR, HR), HR)
@@ -208,7 +215,6 @@
             kvs[d, :, HD:] = values
             go(rc(kvs.at[d], kvbuf.at[v, c], kv_send.at[d], kv_recv.at[v, c],
                   (p, vv * gr + r, c)))
-    weight_step(V - 1)
     key_value_block(0)
 
     for copy in own:
@@ -305,11 +311,15 @@
     for d in range(1, G):
         gg = mod(g + d, G)
         wait_in(sob.at[:, cols(gg, HC)], so_recv.at[gg])
-    self_ref[...] = sob[...]
+    self_copy = pltpu.make_async_copy(sob, self_ref, loc_sem.at[5])
+    self_copy.start()
     for d in range(1, n):
         t = mod(s + d, n)
         wait_in(cob.at[:, cols(t, HD)], co_recv.at[t])
-    cross_ref[...] = cob[...]
+    cross_copy = pltpu.make_async_copy(cob, cross_ref, loc_sem.at[6])
+    cross_copy.start()
+    self_copy.wait()
+    cross_copy.wait()
 
     for copy, when in pending:
         if when is None:
@@ -340,6 +350,7 @@
     HR = ROWS // T
     weight = cross_kv_weight.reshape(FH, 2 * HD)
     vm = pl.BlockSpec(memory_space=pltpu.VMEM)
+    hbm = pl.BlockSpec(memory_space=pl.ANY)
     sm = pl.BlockSpec(memory_space=pltpu.SMEM)
     sem = pltpu.SemaphoreType.DMA
     VM = pltpu.VMEM
@@ -349,8 +360,8 @@
             jax.ShapeDtypeStruct((R, DM), BF16),
             jax.ShapeDtypeStruct((R, DM), BF16),
         ),
-        in_specs=[vm] * 8 + [sm] * 2,
-        out_specs=(vm, vm),
+        in_specs=[hbm] * 4 + [vm, hbm, vm, hbm] + [sm] * 2,
+        out_specs=(hbm, hbm),
         scratch_shapes=[
             VM((V, FH, 2 * HD), BF16),
             VM((gr, CR, FH), BF16),
@@ -377,7 +388,7 @@
             sem((n,)), sem((n,)),
             sem((G,)), sem((G,)),
             sem((n,)), sem((n,)),
-            sem((5,)),
+            sem((7,)),
         ],
         compiler_params=pltpu.CompilerParams(
             collective_id=0, has_side_effects=True, vmem_limit_bytes=56 * 1024 * 1024

time: 80.6 us -> 79.2 us (0.983)
  Pallas kernels: 75 us -> 73.5 us
    pallas_call x1, Pallas kernels: 75 us -> 73.5 us  [per_device(): pl.pallas_call(functools.partial(kernel, (parts, n, T, V)), out_shape=(ja...]
where the time goes in v3:
time: 79.2 us; the launch traced here: 78.9 us
  Pallas kernels  73.5 us (93%)
  local copies, waits for them, and re-layouts  4.76 us (6%)
    pallas_call x1, Pallas kernels, per_device(): pl.pallas_call(functools.partial(kernel, (parts, n, T, V)), out_shape=(ja...  73.5 us
    unnamed x5, local copies, waits for them, and re-layouts  4.76 us

profile of v3, /device:TPU:0, one launch (start us, length us, event | category | flops | bytes accessed | tf_op | source)
XLA Modules:
  0.0 78.9 jit_solution(14993811665716072599)
XLA Ops:
  0.6 2.3 %copy.14 = bf16[256,8,2,128]{3,1,2,0:T(8,128)(2,1)} copy(bf16[256,8,2,128]{3,2,1,0:T(2,128)(2,1)} %bitcast.6) | data formatting | bytes 2097152
  3.0 73.5 %shard_map.113 = (bf16[128,1024]{1,0:T(8,128)(2,1)}, bf16[128,1024]{1,0:T(8,128)(2,1)}) custom-call(bf16[128,1024]{1,0:T(8,128)(2,1)} %q_ref.1, bf16[128,1024]{1,0:T(8,128)(2,1)} %k_ref.1, bf16[128,1024]{1,0:T(8,128)(2,1)} %v_ref.1, bf16[128,1024]{1,0:T(8,128)(2,1)} %cq_ref.1, f32[4,1024]{1,0:T(4,128)} %gains_ref.1, bf16[256,2048]{1,0:T(8,128)(2,1)} %cap_ref.1, ...), custom_call_target="tpu_custom_call" | custom-call | tf_op jit(solution)/shard_map/pallas_call | solution.py:357
  76.5 0.0 copy-start
  76.5 1.7 %copy.17 = bf16[128,1024]{1,0:T(8,128)(2,1)} copy(bf16[128,1024]{1,0:T(8,128)(2,1)} %get-tuple-element.4) | data formatting | bytes 524288
  78.2 0.0 copy-done
  78.2 0.7 copy.18
Async XLA Ops:
  76.5 1.7 %copy-start = (bf16[128,1024]{1,0:T(8,128)(2,1)S(1)}, bf16[128,1024]{1,0:T(8,128)(2,1)}, u32[]{:S(2)}) copy-start(bf16[128,1024]{1,0:T(8,128)(2,1)} %get-tuple-element.5) | copy-start | bytes 786436
